TPU v7x, 1024 devices: a whole 4x4x32 slice. The times are simulated.
1024 devices in a mesh: tower: 2 (over x_lo), blk: 64 (over z, x_hi), mp: 8 (over y, core).
Axes of the slice: x: 4 (x_hi: 2, x_lo: 2; x = x_hi * 2 + x_lo), y: 4, z: 32, core: 2. Of those that a mesh axis runs over, the one named last changes fastest.
Arguments:
- features: bfloat16 [2, 16384, 1152], P('tower', 'blk'), may hold values from -6 to 6
- head: bfloat16 [2, 1152, 1152], P('tower', None, 'mp'), may hold values from -0.1875 to 0.1875
- caption_ids: int32 [16384], replicated, may hold values from 0 to 8191
Outputs:
- head_grad: float32 [2, 1152, 1152], P('tower', 'blk', 'mp')
Inputs may be any that keep to these rules, and one draw needn't show every extreme that they name: `caption_ids`: an image and a text with equal caption ids form a positive pair; ids repeat across pairs.
All inputs are finite; a program needn't handle non-finite values.
Results may differ from a plain program's by a relative error of at most 0.003.
Values may be sent and summed in bfloat16 or wider, within the bound.
A program may use at most 32 MiB of HBM per device.

v0:
```python
import jax
import jax.numpy as jnp
from jax import lax
from jax.sharding import PartitionSpec as P

LOGIT_SCALE = 10.0
LOGIT_BIAS = -5.0


def partner(x, axis, apart):
    return lax.ppermute(x, axis, [(i, i ^ 1 << apart) for i in range(lax.axis_size(axis))])


def per_device(features, head, caption_ids):
    local_rows = features[0]
    own_weights = head[0]
    column_part = lax.optimization_barrier(
        jnp.dot(local_rows, own_weights, preferred_element_type=jnp.float32).astype(jnp.bfloat16)
    )
    projected = lax.all_gather(column_part, "mp", axis=1, tiled=True)
    output_width = projected.shape[1]
    column_width = column_part.shape[1]
    values = projected.astype(jnp.float32)
    norm_factor = lax.rsqrt(jnp.mean(values * values, axis=1, keepdims=True) + 1e-06)
    embedded = (values * norm_factor * output_width ** (-0.5)).astype(jnp.bfloat16)
    slices = lax.axis_size("mp")
    blocks = lax.axis_size("blk")
    slice_index = lax.axis_index("mp")
    block_index = lax.axis_index("blk")
    row_count = embedded.shape[0]
    slice_rows = row_count // slices
    own_slice = lax.dynamic_slice_in_dim(embedded, slice_index * slice_rows, slice_rows, 0)
    partner_slice = partner(own_slice, "tower", 0)
    opposite_tower = lax.all_gather(partner_slice, "blk", axis=0, tiled=True)
    id_table = caption_ids.reshape(blocks, slices, slice_rows)
    partner_ids = lax.dynamic_index_in_dim(id_table, slice_index, 1, keepdims=False).reshape(
        blocks * slice_rows
    )
    own_ids = lax.dynamic_slice_in_dim(caption_ids, block_index * row_count, row_count, 0)
    similarity_logits = (
        LOGIT_SCALE
        * lax.dot_general(
            embedded, opposite_tower, (((1,), (1,)), ((), ())), preferred_element_type=jnp.float32
        )
        + LOGIT_BIAS
    )
    label_signs = jnp.where(own_ids[:, None] == partner_ids[None, :], 1.0, -1.0).astype(jnp.float32)
    matching_weights = (-label_signs * jax.nn.sigmoid(-label_signs * similarity_logits)).astype(
        jnp.bfloat16
    )
    partial_gradient = LOGIT_SCALE * jnp.dot(
        matching_weights, opposite_tower, preferred_element_type=jnp.float32
    )
    gradient = lax.psum(partial_gradient, "mp")
    inner_sum = jnp.sum(values * gradient, axis=1, keepdims=True)
    own_gradient = lax.dynamic_slice_in_dim(gradient, slice_index * column_width, column_width, 1)
    own_values = lax.dynamic_slice_in_dim(values, slice_index * column_width, column_width, 1)
    back_rows = (
        norm_factor * output_width ** (-0.5) * own_gradient
        - norm_factor**3 * inner_sum * output_width ** (-1.5) * own_values
    ).astype(jnp.bfloat16)
    weight_part = lax.dot_general(
        local_rows, back_rows, (((0,), (0,)), ((), ())), preferred_element_type=jnp.float32
    )
    return lax.psum_scatter(weight_part, "blk", scatter_dimension=0, tiled=True)[None]


def solution(mesh):
    in_specs = (P("tower", "blk", None), P("tower", None, "mp"), P())
    out_specs = P("tower", "blk", "mp")
    return jax.shard_map(
        per_device, mesh=mesh, in_specs=in_specs, out_specs=out_specs, check_vma=False
    )
```

profile of v0, /device:TPU:24, one launch (start us, length us, event | category | flops | bytes accessed | tf_op | source)
XLA Modules:
  0.0 1049.8 jit_solution(9104190771881582271)
XLA Ops:
  6.5 0.0 copy-start
  6.5 0.0 all-gather.2.cloned.1.call-start
  6.5 1.1 copy-done
  7.6 0.0 copy-start.1
  7.6 1.3 convolution_convert_fusion
  9.0 23.1 %all_gather.6 = bf16[256,1152]{0,1:T(8,128)(2,1)S(1)} all-gather(bf16[256,144]{0,1:T(8,128)(2,1)S(1)} %convolution_convert_fusion), channel_id=1, replica_groups=mesh['tower'=2,'blk'=64,'mp'=8] {'mp'}, dimensions={1}, use_global_device_ids=true | all-gather | bytes 663552 | tf_op jit(solution)/shard_map/all_gather | solution.py:20
  32.1 0.2 multiply_reduce_fusion.1
  32.3 0.1 multiply_convert_fusion
  32.4 0.2 constant_dynamic-slice_fusion
  32.6 1.9 collective-permute-start
  34.5 9.2 collective-permute-done
  43.7 0.8 copy.8
  44.5 0.0 all-gather.2.cloned.1.call-update
  44.5 0.0 all-reduce.4.cloned.1.call-start
  44.6 0.0 copy-done.1
  44.6 0.1 reshape.30
  44.7 0.1 dynamic-slice_reduce_fusion
  44.8 0.1 eq.16
  44.9 0.1 dynamic_slice.16
  45.0 293.2 %all-gather.2.cloned.1.call-done = bf16[2048,1152]{1,0:T(8,128)(2,1)} async-done(((bf16[32,1152]{1,0:T(8,128)(2,1)}), bf16[2048,1152]{1,0:T(8,128)(2,1)}) %all-gather.2.cloned.1.call-update) | async-done | bytes 4718608 | tf_op jit(solution)/shard_map/all_gather | solution.py:34
  338.2 8.3 convolution_multiply_fusion
  346.5 0.0 all-reduce.4.cloned.1.call-update
  346.6 0.0 all-reduce.6.cloned.1.call-start
  346.6 0.1 convert_element_type.16
  346.7 85.7 %all-reduce.4.cloned.1.call-done = f32[256,1152]{0,1:T(8,128)} async-done(((f32[256,1152]{0,1:T(8,128)}), f32[256,1152]{0,1:T(8,128)}) %all-reduce.4.cloned.1.call-update) | async-done | bytes 1179664 | tf_op jit(solution)/shard_map/psum | solution.py:54
  432.4 1.5 multiply_reduce_fusion
  433.9 2.1 convolution_bitcast_fusion
  436.0 0.0 all-reduce.6.cloned.1.call-update
  436.0 1.3 dynamic-slice
  437.9 603.7 %all-reduce.6.cloned.1.call-done = f32[1152,144]{0,1:T(8,128)} async-done(((f32[1152,144]{0,1:T(8,128)}), f32[1152,144]{0,1:T(8,128)}) %all-reduce.6.cloned.1.call-update) | async-done | bytes 663568
  1041.6 1.0 dynamic-slice_bitcast_fusion
  1042.6 0.7 copy.10
  (2 shorter events, 0.0 us)
Async XLA Ops:
  6.5 1.1 copy-start
  6.5 331.7 %all-gather.2.cloned.1.call-start = ((), (), s32[]{:S(2)}) async-start(), calls=%async_computation | async-start | bytes 4792320 | tf_op jit(solution)/shard_map/all_gather | solution.py:34
  7.6 37.0 %copy-start.1 = (s32[16384]{0:T(1024)S(1)}, s32[16384]{0:T(1024)}, u32[]{:S(2)}) copy-start(s32[16384]{0:T(1024)} %param.5) | copy-start | bytes 196612
  32.6 11.2 %collective-permute-start = (bf16[32,1152]{0,1:T(8,128)(2,1)S(1)}, bf16[32,1152]{0,1:T(8,128)(2,1)S(1)}, u32[]{:S(2)}, u32[]{:S(2)}) collective-permute-start(bf16[32,1152]{0,1:T(8,128)(2,1)S(1)} %constant_dynamic-slice_fusion), channel_id=1, source_target_pairs={{0,512},{512,0},{1,513},{513,1},{2,514},{514,2},{3,515},{515,3},{4... | collective-permute-start | bytes 221192 | tf_op jit(solution)/shard_map/ppermute | solution.py:11
  44.5 387.9 %all-reduce.4.cloned.1.call-start = ((), (), s32[]{:S(2)}) async-start(), calls=%async_computation.1 | async-start | bytes 2359296 | tf_op jit(solution)/shard_map/psum | solution.py:54
  346.6 695.0 %all-reduce.6.cloned.1.call-start = ((), (), s32[]{:S(2)}) async-start(), calls=%async_computation.2 | async-start | bytes 1327104
Sparse Core Ops, SparseCore 0:
  44.7 293.4 all-gather.1
  346.7 85.6 all-reduce.3
  436.1 605.4 all-reduce.5
where the time goes:
time: 1050 us
  waiting for transfers between devices  992 us (94%)
  blocking collectives  23.1 us (2%)
  between operations  13.8 us (1%)
  matrix products  11.7 us (1%)
    unnamed x4, waiting for transfers between devices  604 us
    all_gather x1, waiting for transfers between devices, per_device(): opposite_tower = lax.all_gather(partner_slice, 'blk', axis=0, tiled=True)  293 us
    psum x1, waiting for transfers between devices, per_device(): gradient = lax.psum(partial_gradient, 'mp')  85.7 us
    all_gather x1, blocking collectives, per_device(): projected = lax.all_gather(column_part, 'mp', axis=1, tiled=True)  23.1 us
  transfers between devices with their start and end apart: 4, of which 4 were waited for; matrix products, arithmetic and copies ran while one was open for 0% of the time, Pallas kernels for 0%

commit v1 on v0

v1 whole, which is shorter than its diff:
```python
import jax
import jax.numpy as jnp
from jax import lax
from jax.experimental import pallas as pl
from jax.experimental.pallas import tpu as pltpu
from jax.sharding import PartitionSpec as P

MESH = pl.DeviceIdType.MESH
DMA = pltpu.SemaphoreType.DMA
F32, BF16 = jnp.float32, jnp.bfloat16

LOGIT_SCALE = 10.0
LOGIT_BIAS = -5.0
D = E = 1152
ROWS = 256
NZ, NY, NM = 32, 4, 8
SL = ROWS // NM
CH = 2 * SL
COLS = E // NM
STRIP = D // (2 * NZ)
PAD = 24
SUB = 4
SR = CH // SUB
HOPS = NZ // 2
INV = E ** -0.5


def copy_to(src, dst, send, recv, target):
    return pltpu.make_async_remote_copy(
        src_ref=src, dst_ref=dst, send_sem=send, recv_sem=recv, device_id=target, device_id_type=MESH
    )


def kernel(f_ref, h_ref, ids_ref, out_ref,
           wide, pieces, opp_in, own_in, ring, own_rows, own_emb, own_proj, opp_ids, own_ids,
           grad, grad_out, grad_in, strips, strips_out, back_out, back_in, part_out, part_in,
           proj_s, proj_r, emb_s, emb_r, ring_s, ring_r, sib_s, sib_r, strip_s, strip_r,
           grad_s, grad_r, back_s, back_r, part_s, part_r):
    k = lax.axis_index("tower")
    b = lax.axis_index("blk")
    m = lax.axis_index("mp")
    z, xh = b // 2, lax.rem(b, 2)
    y, c = m // 2, lax.rem(m, 2)
    q = xh * NM + m

    def at(tower, plane, half, unit):
        return (tower, plane * 2 + half, unit)

    def in_plane(d):
        other = lax.rem(q + d, 2 * NM)
        return other // NM, lax.rem(other, NM)

    sibling = at(k, z, xh, m + 1 - 2 * c)
    after = at(k, lax.rem(z + 1 + (NZ - 2) * c, NZ), xh, m)
    before = at(k, lax.rem(z + NZ - 1 - (NZ - 2) * c, NZ), xh, m)

    barrier = pltpu.get_barrier_semaphore()

    def greet(target):
        pl.semaphore_signal(barrier, inc=1, device_id=target, device_id_type=MESH)

    def greet_plane(d, carry):
        half, unit = in_plane(d)
        greet(at(k, z, half, unit))
        return carry

    def greet_tower(j, carry):
        greet(at(1 - k, z, xh, j))
        return carry

    def greet_far(d, carry):
        greet(at(k, lax.rem(z + d, NZ), xh, m))
        return carry

    greet(after)
    greet(before)
    lax.fori_loop(1, 2 * NM, greet_plane, 0)
    lax.fori_loop(0, NM, greet_tower, 0)

    wide[...] = jnp.zeros_like(wide)
    wide[:, 0:COLS] = jnp.dot(f_ref[...], h_ref[...], preferred_element_type=F32)
    shifted = pltpu.roll(wide[...], (COLS - 128) * m, 1)
    pieces[...] = shifted.astype(BF16).reshape(NM, SL, 256)
    pl.semaphore_wait(barrier, 2 * NM - 1 + NM + 2)

    def opp_copy(d):
        j = lax.rem(m + d, NM)
        return copy_to(pieces.at[j], opp_in.at[m], proj_s.at[0, d], proj_r.at[0, d], at(1 - k, z, xh, j))

    def own_copy(d):
        j = lax.rem(m + d, NM)
        return copy_to(pieces.at[j], own_in.at[m], proj_s.at[1, d], proj_r.at[1, d], at(k, z, xh, j))

    def send_opp(d, carry):
        opp_copy(d).start()
        return carry

    def send_own(d, carry):
        own_copy(d).start()
        return carry

    lax.fori_loop(0, NM, send_opp, 0)
    lax.fori_loop(1, NM, send_own, 0)
    own_in[m] = pieces[m]

    lane = lax.broadcasted_iota(jnp.int32, (1, 128), 1)
    odd = lax.rem(y, 2) == 1

    def id_row(plane):
        return ids_ref[pl.ds(plane * 4 + xh * 2 + y // 2, 1), :]

    def fill_ids(p, carry):
        left = id_row(lax.rem(z + p, NZ))
        right = id_row(lax.rem(z + NZ - 1 - p, NZ))
        low = jnp.where(odd, pltpu.roll(left, 64, 1), left)
        high = jnp.where(odd, right, pltpu.roll(right, 64, 1))
        opp_ids[pl.ds(p, 1), :] = jnp.where(lane < 64, low, high)
        return carry

    lax.fori_loop(0, HOPS, fill_ids, 0)
    for half in range(2):
        row = ids_ref[pl.ds(z * 4 + 2 * c + half, 1), :]
        own_ids[half * 128:(half + 1) * 128, :] = jnp.broadcast_to(row, (128, 128)).T

    def assemble(slots):
        tiles = [slots[0, :, 0:128]]
        for t in range(1, NM):
            tiles.append(slots[t, :, 0:128] + slots[t - 1, :, 128:256])
        tiles.append(slots[NM - 1, :, 128:256])
        return jnp.concatenate(tiles, axis=1)

    def norm_of(values):
        return lax.rsqrt(jnp.mean(values * values, axis=1, keepdims=True) + 1e-06)

    def embed(projected):
        values = projected.astype(F32)
        return (values * norm_of(values) * INV).astype(BF16)

    def recv_opp(d, carry):
        opp_copy(d).wait_recv()
        return carry

    def recv_own(d, carry):
        own_copy(d).wait_recv()
        return carry

    def slot(s):
        return jnp.maximum(2 * s - 1 + c, 0)

    def hop(s, i):
        rows = pl.ds(pl.multiple_of(i * SR, SR), SR)
        return copy_to(ring.at[slot(s), rows], ring.at[slot(s + 1), rows], ring_s.at[s, i], ring_r.at[s, i], after)

    def share(s):
        return copy_to(ring.at[slot(s)], ring.at[slot(s)], sib_s.at[s], sib_r.at[s], sibling)

    def share_half(s, index):
        rows = pl.ds(pl.multiple_of(c * SL, SL), SL)
        return copy_to(ring.at[index, rows], ring.at[index, rows], sib_s.at[s], sib_r.at[s], sibling)

    def order(i):
        return lax.rem(2 * c + i, SUB)

    lax.fori_loop(0, NM, recv_opp, 0)
    ring[0, pl.ds(pl.multiple_of(c * SL, SL), SL), :] = embed(assemble(opp_in))
    share_half(0, 0).start()
    hop(0, order(0)).start()
    hop(0, order(1)).start()

    lax.fori_loop(1, NM, recv_own, 0)
    own_proj[...] = assemble(own_in)
    own_rows[...] = embed(own_proj[...])

    share_half(0, 0).wait_recv()
    hop(0, order(2)).start()
    hop(0, order(3)).start()

    def emb_copy(dx, dy):
        target = at(k, z, lax.rem(xh + dx, 2), lax.rem(y + dy, NY) * 2 + xh)
        return copy_to(own_rows, own_emb.at[m], emb_s.at[dx, dy], emb_r.at[c, dy], target)

    def emb_wait(core, dy):
        copy_to(own_rows, own_emb.at[0], emb_s.at[0, 0], emb_r.at[core, dy], sibling).wait_recv()

    mine = c == xh

    @pl.when(mine)
    def _():
        own_emb[m] = own_rows[...]

    @pl.when(jnp.logical_not(mine))
    def _():
        emb_copy(0, 0).start()

    for dy in range(1, NY):
        emb_copy(0, dy).start()
    for dy in range(NY):
        emb_copy(1, dy).start()

    def strip_columns(half):
        for part in range(3):
            n = lax.broadcasted_iota(jnp.int32, (256, 1), 0) + part * 256
            plane = (n * 2731) >> 16
            r = n - plane * PAD
            wanted = jnp.where(r < STRIP, plane * (2 * STRIP) + half * STRIP + r, -1)
            pick = (lax.broadcasted_iota(jnp.int32, (256, D), 1) == wanted).astype(BF16)
            yield part, lax.dot_general(
                pick, f_ref[...], (((1,), (1,)), ((), ())), preferred_element_type=F32
            ).astype(BF16)

    for part, value in strip_columns(1 - xh):
        strips_out[part * 256:(part + 1) * 256, :] = value
    strip_copy = copy_to(strips_out, strips.at[1], strip_s, strip_r, at(k, z, 1 - xh, m))
    strip_copy.start()
    for part, value in strip_columns(xh):
        strips[0, part * 256:(part + 1) * 256, :] = value
    grad[...] = jnp.zeros_like(grad)

    def emb_ready():
        for core in range(2):
            for dy in range(NY):
                if dy == 0:
                    @pl.when(jnp.logical_not(jnp.logical_and(mine, core == c)))
                    def _(core=core):
                        emb_wait(core, 0)
                else:
                    emb_wait(core, dy)

    def forward(s):
        for i in range(SUB):
            hop(s - 1, order(i)).wait_recv()
            hop(s, order(i)).start()
        share(s).start()

    def batch(j):
        opposite = ring[pl.ds(4 * j, 4)].reshape(4 * CH, E)
        own = own_emb[...].reshape(ROWS, E)
        logits = LOGIT_SCALE * lax.dot_general(
            own, opposite, (((1,), (1,)), ((), ())), preferred_element_type=F32
        ) + LOGIT_BIAS
        partner = opp_ids[pl.ds(2 * j, 2), :]
        same = jnp.concatenate([own_ids[...] == partner[0:1], own_ids[...] == partner[1:2]], axis=1)
        sign = jnp.where(same, 1.0, -1.0)
        weights = (-sign / (1.0 + jnp.exp(sign * logits))).astype(BF16)
        grad[...] += jnp.dot(weights, opposite, preferred_element_type=F32)

    forward(1)
    forward(2)
    emb_ready()

    def two_hops(t, carry):
        forward(2 * t + 1)
        share(2 * t - 1).wait_recv()
        share(2 * t).wait_recv()
        batch(t - 1)
        forward(2 * t + 2)
        return carry

    lax.fori_loop(1, HOPS // 2 - 1, two_hops, 0)

    last = HOPS - 1

    def last_hop(i):
        rows = pl.ds(pl.multiple_of(i * SR, SR), SR)
        return copy_to(ring.at[slot(last), rows], ring.at[2 * HOPS - 1, rows],
                       ring_s.at[last, i], ring_r.at[last, i], after)

    for i in range(SUB):
        hop(last - 1, order(i)).wait_recv()
        if i < SUB // 2:
            last_hop(order(i)).start()
    share(last).start()
    share(last - 2).wait_recv()
    share(last - 1).wait_recv()
    batch(HOPS // 2 - 2)
    for i in range(SUB // 2):
        last_hop(order(i)).wait_recv()
    share_half(HOPS, 2 * HOPS - 1).start()
    share(last).wait_recv()
    share_half(HOPS, 2 * HOPS - 1).wait_recv()
    batch(HOPS // 2 - 1)

    grad_out[...] = (LOGIT_SCALE * grad[...]).astype(BF16).reshape(NM, SL, E)

    def grad_copy(core, dy):
        unit = lax.rem(y + dy, NY) * 2 + core
        return copy_to(grad_out.at[unit], grad_in.at[xh * NY + dy], grad_s.at[core, dy],
                       grad_r.at[xh, dy], at(k, z, c, unit))

    def grad_wait(half, dy):
        copy_to(grad_out.at[0], grad_in.at[0], grad_s.at[0, 0], grad_r.at[half, dy], sibling).wait_recv()

    def grad_all(act):
        for dy in (2, 1, 3, 0):
            for core in range(2):
                if dy == 0:
                    @pl.when(jnp.logical_not(jnp.logical_and(mine, core == c)))
                    def _(core=core):
                        act(grad_copy(core, 0))
                else:
                    act(grad_copy(core, dy))

    grad_all(lambda copy: copy.start())

    @pl.when(mine)
    def _():
        grad_in[xh * NY] = grad_out[m]

    values = own_proj[...].astype(F32)
    norm = norm_of(values)
    for half in range(2):
        for dy in range(NY):
            if dy == 0:
                @pl.when(jnp.logical_not(jnp.logical_and(mine, xh == half)))
                def _(half=half):
                    grad_wait(half, 0)
            else:
                grad_wait(half, dy)
    gradient = grad_in[0].astype(F32)
    for i in range(1, 2 * NY):
        gradient = gradient + grad_in[i].astype(F32)

    inner = jnp.sum(values * gradient, axis=1, keepdims=True)
    back = (norm * INV * gradient - norm ** 3 * inner * E ** -1.5 * values).astype(BF16)
    for t in range(NM):
        back_out[t] = back[:, t * 128:t * 128 + 256]

    def back_copy(d):
        half, unit = in_plane(d)
        return copy_to(back_out.at[unit], back_in.at[q], back_s.at[d], back_r.at[d], at(k, z, half, unit))

    def send_back(d, carry):
        back_copy(d).start()
        return carry

    def recv_back(d, carry):
        back_copy(d).wait_recv()
        return carry

    lax.fori_loop(1, 2 * NM, send_back, 0)
    back_in[q] = back_out[m]
    strip_copy.wait_recv()
    lax.fori_loop(1, 2 * NM, recv_back, 0)

    own_back = back_in[pl.ds(xh * NM, NM)].reshape(ROWS, 256)
    other_back = back_in[pl.ds((1 - xh) * NM, NM)].reshape(ROWS, 256)
    head_part = jnp.dot(strips[0], own_back, preferred_element_type=F32)
    head_part += jnp.dot(strips[1], other_back, preferred_element_type=F32)
    head_part = pltpu.roll(head_part, lax.rem(256 - (COLS - 128) * m, 256), 1)
    extra = jnp.where(lane < COLS - 128, head_part[:, 128:256], 0.0)
    extra = pltpu.roll(extra, 0, 1, stride=COLS - 128, stride_axis=0)
    extra = jnp.sum(extra.reshape(NZ, PAD // 8, 8, 128), axis=2)
    packed = head_part[:, 0:128].reshape(NZ, PAD, 128)
    r = lax.broadcasted_iota(jnp.int32, (NZ, PAD, 128), 1)
    for g in range(PAD // 8):
        packed = jnp.where(r == STRIP + g, extra[:, g:g + 1, :], packed)
    part_out[:, 0:PAD, :] = packed.astype(BF16)
    part_out[:, PAD:32, :] = jnp.zeros((NZ, 32 - PAD, 128), BF16)

    def part_copy(d):
        plane = lax.rem(z + d, NZ)
        return copy_to(part_out.at[plane], part_in.at[d], part_s.at[d], part_r.at[d], at(k, plane, xh, m))

    def send_part(i, carry):
        part_copy(HOPS - i).start()

        @pl.when(i > 0)
        def _():
            part_copy(HOPS + i).start()
        return carry

    def recv_part(d, carry):
        part_copy(d).wait_recv()
        return carry

    lax.fori_loop(0, HOPS, send_part, 0)
    part_in[0] = part_out[z]
    lax.fori_loop(1, NZ, recv_part, 0)
    total = part_in[0].astype(F32)
    for d in range(1, NZ):
        total = total + part_in[d].astype(F32)
    out_ref[:, 0:128] = total[0:STRIP, :]
    spread = jnp.concatenate(
        [jnp.broadcast_to(total[STRIP + g:STRIP + g + 1, :], (8, 128)) for g in range(PAD // 8)], axis=0
    )
    row = lax.rem(lax.broadcasted_iota(jnp.int32, (PAD, 128), 0), 8)
    tail = spread
    for j in range(1, 8):
        tail = jnp.where(row == j, pltpu.roll(spread, 128 - (COLS - 128) * j, 1), tail)
    out_ref[:, 128:COLS] = tail[0:STRIP, 0:COLS - 128]

    def sent_proj(d, carry):
        opp_copy(d).wait_send()

        @pl.when(d > 0)
        def _():
            own_copy(d).wait_send()
        return carry

    def sent_hops(s, carry):
        for i in range(SUB):
            hop(s, i).wait_send()
        share(s + 1).wait_send()
        return carry

    def sent_back(d, carry):
        back_copy(d).wait_send()
        return carry

    def sent_part(d, carry):
        part_copy(d).wait_send()
        return carry

    lax.fori_loop(0, NM, sent_proj, 0)
    share_half(0, 0).wait_send()
    lax.fori_loop(0, last, sent_hops, 0)
    for i in range(SUB // 2):
        last_hop(order(i)).wait_send()
    share_half(HOPS, 2 * HOPS - 1).wait_send()

    @pl.when(jnp.logical_not(mine))
    def _():
        emb_copy(0, 0).wait_send()

    for dy in range(1, NY):
        emb_copy(0, dy).wait_send()
    for dy in range(NY):
        emb_copy(1, dy).wait_send()
    strip_copy.wait_send()
    grad_all(lambda copy: copy.wait_send())
    lax.fori_loop(1, 2 * NM, sent_back, 0)
    lax.fori_loop(1, NZ, sent_part, 0)


def per_device(features, head, caption_ids):
    vmem = pl.BlockSpec(memory_space=pltpu.VMEM)
    flops = 2 * ROWS * D * COLS + 4 * ROWS * NZ * CH * E + 4 * NZ * PAD * ROWS * 256
    out = pl.pallas_call(
        kernel,
        out_shape=jax.ShapeDtypeStruct((STRIP, COLS), F32),
        in_specs=[vmem] * 3,
        out_specs=vmem,
        scratch_shapes=[
            pltpu.VMEM((ROWS, 256), F32),
            pltpu.VMEM((NM, SL, 256), BF16),
            pltpu.VMEM((NM, SL, 256), BF16),
            pltpu.VMEM((NM, SL, 256), BF16),
            pltpu.VMEM((NZ, CH, E), BF16),
            pltpu.VMEM((SL, E), BF16),
            pltpu.VMEM((NM, SL, E), BF16),
            pltpu.VMEM((SL, E), BF16),
            pltpu.VMEM((HOPS, 128), jnp.int32),
            pltpu.VMEM((ROWS, 128), jnp.int32),
            pltpu.VMEM((ROWS, E), F32),
            pltpu.VMEM((NM, SL, E), BF16),
            pltpu.VMEM((2 * NY, SL, E), BF16),
            pltpu.VMEM((2, NZ * PAD, ROWS), BF16),
            pltpu.VMEM((NZ * PAD, ROWS), BF16),
            pltpu.VMEM((NM, SL, 256), BF16),
            pltpu.VMEM((2 * NM, SL, 256), BF16),
            pltpu.VMEM((NZ, 32, 128), BF16),
            pltpu.VMEM((NZ, 32, 128), BF16),
            DMA((2, NM)), DMA((2, NM)),
            DMA((2, NY)), DMA((2, NY)),
            DMA((HOPS, SUB)), DMA((HOPS, SUB)),
            DMA((HOPS + 1,)), DMA((HOPS + 1,)),
            DMA, DMA,
            DMA((2, NY)), DMA((2, NY)),
            DMA((2 * NM,)), DMA((2 * NM,)),
            DMA((NZ,)), DMA((NZ,)),
        ],
        compiler_params=pltpu.CompilerParams(
            collective_id=0, has_side_effects=True, vmem_limit_bytes=40 << 20
        ),
        cost_estimate=pl.CostEstimate(flops=flops, bytes_accessed=2 << 20, transcendentals=ROWS * NZ * CH),
    )(features[0], head[0], caption_ids.reshape(128, 128))
    return out[None]


def solution(mesh):
    in_specs = (P("tower", "blk", None), P("tower", None, "mp"), P())
    out_specs = P("tower", "blk", "mp")
    return jax.shard_map(
        per_device, mesh=mesh, in_specs=in_specs, out_specs=out_specs, check_vma=False
    )
```

time: 1050 us -> 129 us (0.12)
  waiting for transfers between devices: 992 us -> 0 us
  Pallas kernels: 0 us -> 126 us
  blocking collectives: 23.1 us -> 0 us
  between operations: 13.8 us -> 0.03 us
  matrix products: 11.7 us -> 0 us
    unnamed x4 -> x0, waiting for transfers between devices: 604 us -> none
    all_gather x1 -> x0, waiting for transfers between devices: 293 us -> none  [per_device(): opposite_tower = lax.all_gather(partner_slice, 'blk', axis=0, tiled=True)]
    pallas_call x0 -> x1, Pallas kernels: none -> 126 us  [per_device(): pl.pallas_call(kernel, out_shape=jax.ShapeDtypeStruct((STRIP, COLS), F32)...]
    psum x1 -> x0, waiting for transfers between devices: 85.7 us -> none  [per_device(): gradient = lax.psum(partial_gradient, 'mp')]
    all_gather x1 -> x0, blocking collectives: 23.1 us -> none  [per_device(): projected = lax.all_gather(column_part, 'mp', axis=1, tiled=True)]
    dot_general x3 -> x0, matrix products: 11.7 us -> none  [the longest x1 8.33 us: per_device(): jnp.dot(matching_weights, opposite_tower, preferred_element_type=jnp.floa...]
  transfers between devices with their start and end apart: 4 -> 0, of which waited for: 4 -> 0; matrix products, arithmetic and copies ran while one was open for 0% -> 0% of each run, Pallas kernels for 0% -> 0%
where the time goes in v1:
time: 129 us; the launch traced here: 128 us
  Pallas kernels  126 us (98%)
  local copies, waits for them, and re-layouts  1.91 us (1%)
    pallas_call x1, Pallas kernels, per_device(): pl.pallas_call(kernel, out_shape=jax.ShapeDtypeStruct((STRIP, COLS), F32)...  126 us

profile of v1, /device:TPU:24, one launch (start us, length us, event | category | flops | bytes accessed | tf_op | source)
XLA Modules:
  0.0 128.2 jit_solution(7939471680652396982)
XLA Ops:
  0.0 0.0 copy-start
  0.0 0.0 copy-start.1
  0.0 1.3 copy.4
  1.3 0.0 copy-done
  1.3 0.0 copy-done.1
  1.3 126.2 %shard_map.37 = f32[18,144]{1,0:T(8,128)S(1)} custom-call(bf16[256,1152]{1,0:T(8,128)(2,1)S(1)} %bitcast.6, bf16[1152,144]{1,0:T(8,128)(2,1)S(1)} %bitcast.4, s32[128,128]{1,0:T(8,128)S(1)} %bitcast.7), custom_call_target="tpu_custom_call" | custom-call | flops 2702180352 | bytes 2097152 | tf_op jit(solution)/shard_map/pallas_call | solution.py:438
  127.5 0.6 copy.5
Async XLA Ops:
  0.0 1.3 %copy-start = (bf16[1,256,1152]{2,1,0:T(8,128)(2,1)S(1)}, bf16[1,256,1152]{2,1,0:T(8,128)(2,1)}, u32[]{:S(2)}) copy-start(bf16[1,256,1152]{2,1,0:T(8,128)(2,1)} %param.3) | copy-start | bytes 1769476
  0.0 1.3 %copy-start.1 = (s32[16384]{0:T(1024)S(1)}, s32[16384]{0:T(1024)}, u32[]{:S(2)}) copy-start(s32[16384]{0:T(1024)} %param.5) | copy-start | bytes 196612

commit v2 on v1

--- a/solution.py
+++ b/solution.py
@@ -22,6 +22,9 @@
 SUB = 4
 SR = CH // SUB
 HOPS = NZ // 2
+JUMP = 4
+GROUP = 4
+GROUPS = NZ // GROUP
 INV = E ** -0.5
 
 
@@ -32,10 +35,11 @@
 
 
 def kernel(f_ref, h_ref, ids_ref, out_ref,
-           wide, pieces, opp_in, own_in, ring, own_rows, own_emb, own_proj, opp_ids, own_ids,
+           rows_in, head_in, ids_in, pieces, opp_in, own_in, ring, own_rows, own_emb, own_proj, opp_ids, own_ids,
            grad, grad_out, grad_in, strips, strips_out, back_out, back_in, part_out, part_in,
-           proj_s, proj_r, emb_s, emb_r, ring_s, ring_r, sib_s, sib_r, strip_s, strip_r,
-           grad_s, grad_r, back_s, back_r, part_s, part_r):
+           sum_out, sum_in,
+           in_s, proj_s, proj_r, emb_s, emb_r, ring_s, ring_r, sib_s, sib_r, strip_s, strip_r,
+           grad_s, grad_r, back_s, back_r, part_s, part_r, sum_s, sum_r):
     k = lax.axis_index("tower")
     b = lax.axis_index("blk")
     m = lax.axis_index("mp")
@@ -53,6 +57,8 @@
     sibling = at(k, z, xh, m + 1 - 2 * c)
     after = at(k, lax.rem(z + 1 + (NZ - 2) * c, NZ), xh, m)
     before = at(k, lax.rem(z + NZ - 1 - (NZ - 2) * c, NZ), xh, m)
+    ahead = at(k, lax.rem(z + JUMP + (NZ - 2 * JUMP) * c, NZ), xh, m)
+    behind = at(k, lax.rem(z + NZ - JUMP - (NZ - 2 * JUMP) * c, NZ), xh, m)
 
     barrier = pltpu.get_barrier_semaphore()
 
@@ -68,20 +74,27 @@
         greet(at(1 - k, z, xh, j))
         return carry
 
-    def greet_far(d, carry):
-        greet(at(k, lax.rem(z + d, NZ), xh, m))
-        return carry
-
     greet(after)
     greet(before)
+    greet(ahead)
+    greet(behind)
     lax.fori_loop(1, 2 * NM, greet_plane, 0)
     lax.fori_loop(0, NM, greet_tower, 0)
 
-    wide[...] = jnp.zeros_like(wide)
-    wide[:, 0:COLS] = jnp.dot(f_ref[...], h_ref[...], preferred_element_type=F32)
-    shifted = pltpu.roll(wide[...], (COLS - 128) * m, 1)
-    pieces[...] = shifted.astype(BF16).reshape(NM, SL, 256)
-    pl.semaphore_wait(barrier, 2 * NM - 1 + NM + 2)
+    shift = (COLS - 128) * m
+    rows_copy = pltpu.make_async_copy(f_ref, rows_in, in_s.at[0])
+    rows_copy.start()
+    ids_copy = pltpu.make_async_copy(ids_ref, ids_in, in_s.at[1])
+    ids_copy.start()
+    head_in[...] = jnp.zeros_like(head_in)
+    head_copy = pltpu.make_async_copy(h_ref, head_in.at[pl.ds(pl.multiple_of(shift, 16), COLS)], in_s.at[2])
+    head_copy.start()
+    rows_copy.wait()
+    head_copy.wait()
+    pieces[...] = lax.dot_general(
+        rows_in[...], head_in[...], (((1,), (1,)), ((), ())), preferred_element_type=F32
+    ).astype(BF16).reshape(NM, SL, 256)
+    pl.semaphore_wait(barrier, 2 * NM - 1 + NM + 4)
 
     def opp_copy(d):
         j = lax.rem(m + d, NM)
@@ -107,7 +120,7 @@
     odd = lax.rem(y, 2) == 1
 
     def id_row(plane):
-        return ids_ref[pl.ds(plane * 4 + xh * 2 + y // 2, 1), :]
+        return ids_in[pl.ds(plane * 4 + xh * 2 + y // 2, 1), :]
 
     def fill_ids(p, carry):
         left = id_row(lax.rem(z + p, NZ))
@@ -117,9 +130,10 @@
         opp_ids[pl.ds(p, 1), :] = jnp.where(lane < 64, low, high)
         return carry
 
+    ids_copy.wait()
     lax.fori_loop(0, HOPS, fill_ids, 0)
     for half in range(2):
-        row = ids_ref[pl.ds(z * 4 + 2 * c + half, 1), :]
+        row = ids_in[pl.ds(z * 4 + 2 * c + half, 1), :]
         own_ids[half * 128:(half + 1) * 128, :] = jnp.broadcast_to(row, (128, 128)).T
 
     def assemble(slots):
@@ -151,6 +165,10 @@
         rows = pl.ds(pl.multiple_of(i * SR, SR), SR)
         return copy_to(ring.at[slot(s), rows], ring.at[slot(s + 1), rows], ring_s.at[s, i], ring_r.at[s, i], after)
 
+    def jump(i):
+        rows = pl.ds(pl.multiple_of(i * SR, SR), SR)
+        return copy_to(ring.at[0, rows], ring.at[slot(JUMP), rows], ring_s.at[JUMP - 1, i], ring_r.at[JUMP - 1, i], ahead)
+
     def share(s):
         return copy_to(ring.at[slot(s)], ring.at[slot(s)], sib_s.at[s], sib_r.at[s], sibling)
 
@@ -164,6 +182,8 @@
     lax.fori_loop(0, NM, recv_opp, 0)
     ring[0, pl.ds(pl.multiple_of(c * SL, SL), SL), :] = embed(assemble(opp_in))
     share_half(0, 0).start()
+    jump(order(0)).start()
+    jump(order(1)).start()
     hop(0, order(0)).start()
     hop(0, order(1)).start()
 
@@ -172,6 +192,8 @@
     own_rows[...] = embed(own_proj[...])
 
     share_half(0, 0).wait_recv()
+    jump(order(2)).start()
+    jump(order(3)).start()
     hop(0, order(2)).start()
     hop(0, order(3)).start()
 
@@ -200,12 +222,13 @@
     def strip_columns(half):
         for part in range(3):
             n = lax.broadcasted_iota(jnp.int32, (256, 1), 0) + part * 256
-            plane = (n * 2731) >> 16
-            r = n - plane * PAD
+            place = (n * 2731) >> 16
+            r = n - place * PAD
+            plane = (place & (GROUPS - 1)) * GROUP + (place >> 3)
             wanted = jnp.where(r < STRIP, plane * (2 * STRIP) + half * STRIP + r, -1)
             pick = (lax.broadcasted_iota(jnp.int32, (256, D), 1) == wanted).astype(BF16)
             yield part, lax.dot_general(
-                pick, f_ref[...], (((1,), (1,)), ((), ())), preferred_element_type=F32
+                pick, rows_in[...], (((1,), (1,)), ((), ())), preferred_element_type=F32
             ).astype(BF16)
 
     for part, value in strip_columns(1 - xh):
@@ -230,6 +253,11 @@
         for i in range(SUB):
             hop(s - 1, order(i)).wait_recv()
             hop(s, order(i)).start()
+        share(s).start()
+
+    def end_of_chain(s):
+        for i in range(SUB):
+            hop(s - 1, order(i)).wait_recv()
         share(s).start()
 
     def batch(j):
@@ -244,19 +272,33 @@
         weights = (-sign / (1.0 + jnp.exp(sign * logits))).astype(BF16)
         grad[...] += jnp.dot(weights, opposite, preferred_element_type=F32)
 
-    forward(1)
-    forward(2)
+    for t in range(1, JUMP):
+        if t < JUMP - 1:
+            forward(t)
+        else:
+            end_of_chain(t)
+        forward(JUMP - 1 + t)
     emb_ready()
 
-    def two_hops(t, carry):
-        forward(2 * t + 1)
-        share(2 * t - 1).wait_recv()
-        share(2 * t).wait_recv()
-        batch(t - 1)
-        forward(2 * t + 2)
-        return carry
-
-    lax.fori_loop(1, HOPS // 2 - 1, two_hops, 0)
+    def arrived(j):
+        share(2 * j + 1).wait_recv()
+        share(2 * j + 2).wait_recv()
+
+    def one_hop(t, carry):
+        forward(JUMP - 1 + t)
+        arrived(t - JUMP)
+        batch(t - JUMP)
+        return carry
+
+    def two_hops(u, carry):
+        forward(2 * u + JUMP - 1)
+        arrived(u)
+        batch(u)
+        forward(2 * u + JUMP)
+        return carry
+
+    lax.fori_loop(JUMP, 2 * JUMP, one_hop, 0)
+    lax.fori_loop(JUMP, HOPS // 2 - 2, two_hops, 0)
 
     last = HOPS - 1
 
@@ -270,8 +312,7 @@
         if i < SUB // 2:
             last_hop(order(i)).start()
     share(last).start()
-    share(last - 2).wait_recv()
-    share(last - 1).wait_recv()
+    arrived(HOPS // 2 - 2)
     batch(HOPS // 2 - 2)
     for i in range(SUB // 2):
         last_hop(order(i)).wait_recv()
@@ -354,31 +395,76 @@
     r = lax.broadcasted_iota(jnp.int32, (NZ, PAD, 128), 1)
     for g in range(PAD // 8):
         packed = jnp.where(r == STRIP + g, extra[:, g:g + 1, :], packed)
-    part_out[:, 0:PAD, :] = packed.astype(BF16)
-    part_out[:, PAD:32, :] = jnp.zeros((NZ, 32 - PAD, 128), BF16)
+    part_out[:, :, 0:PAD, :] = packed.astype(BF16).reshape(GROUP, GROUPS, PAD, 128)
+    part_out[:, :, PAD:32, :] = jnp.zeros((GROUP, GROUPS, 32 - PAD, 128), BF16)
+
+    low, high = lax.rem(z, GROUP), z // GROUP
 
     def part_copy(d):
-        plane = lax.rem(z + d, NZ)
-        return copy_to(part_out.at[plane], part_in.at[d], part_s.at[d], part_r.at[d], at(k, plane, xh, m))
-
-    def send_part(i, carry):
-        part_copy(HOPS - i).start()
-
-        @pl.when(i > 0)
+        place = lax.rem(low + d, GROUP)
+        return copy_to(part_out.at[place], part_in.at[d - 1], part_s.at[d], part_r.at[d],
+                       at(k, high * GROUP + place, xh, m))
+
+    def sum_copy(d):
+        place = lax.rem(high + d, GROUPS)
+        return copy_to(sum_out.at[place], sum_in.at[d], sum_s.at[d], sum_r.at[d],
+                       at(k, place * GROUP + low, xh, m))
+
+    def sent_proj(d, carry):
+        opp_copy(d).wait_send()
+
+        @pl.when(d > 0)
         def _():
-            part_copy(HOPS + i).start()
-        return carry
-
-    def recv_part(d, carry):
+            own_copy(d).wait_send()
+        return carry
+
+    def sent_hops(s, carry):
+        for i in range(SUB):
+            hop(s, i).wait_send()
+        share(s + 1).wait_send()
+        return carry
+
+    def sent_back(d, carry):
+        back_copy(d).wait_send()
+        return carry
+
+    for d in (2, 1, 3):
+        part_copy(d).start()
+    lax.fori_loop(0, NM, sent_proj, 0)
+    share_half(0, 0).wait_send()
+    lax.fori_loop(0, last, sent_hops, 0)
+    for i in range(SUB // 2):
+        last_hop(order(i)).wait_send()
+    share_half(HOPS, 2 * HOPS - 1).wait_send()
+
+    @pl.when(jnp.logical_not(mine))
+    def _():
+        emb_copy(0, 0).wait_send()
+
+    for dy in range(1, NY):
+        emb_copy(0, dy).wait_send()
+    for dy in range(NY):
+        emb_copy(1, dy).wait_send()
+    strip_copy.wait_send()
+    grad_all(lambda copy: copy.wait_send())
+    lax.fori_loop(1, 2 * NM, sent_back, 0)
+    own_part = part_out[low].astype(F32)
+    for d in (1, 3, 2):
         part_copy(d).wait_recv()
-        return carry
-
-    lax.fori_loop(0, HOPS, send_part, 0)
-    part_in[0] = part_out[z]
-    lax.fori_loop(1, NZ, recv_part, 0)
-    total = part_in[0].astype(F32)
-    for d in range(1, NZ):
-        total = total + part_in[d].astype(F32)
+    summed = own_part
+    for d in range(GROUP - 1):
+        summed = summed + part_in[d].astype(F32)
+    sum_out[...] = summed.astype(BF16)
+    for d in (4, 3, 5, 2, 6, 1, 7):
+        sum_copy(d).start()
+    for d in range(1, GROUP):
+        part_copy(d).wait_send()
+    for d in range(1, GROUPS):
+        sum_copy(d).wait_send()
+    total = sum_out[high].astype(F32)
+    for d in (1, 7, 2, 6, 3, 5, 4):
+        sum_copy(d).wait_recv()
+        total = total + sum_in[d].astype(F32)
     out_ref[:, 0:128] = total[0:STRIP, :]
     spread = jnp.concatenate(
         [jnp.broadcast_to(total[STRIP + g:STRIP + g + 1, :], (8, 128)) for g in range(PAD // 8)], axis=0
@@ -389,48 +475,6 @@
         tail = jnp.where(row == j, pltpu.roll(spread, 128 - (COLS - 128) * j, 1), tail)
     out_ref[:, 128:COLS] = tail[0:STRIP, 0:COLS - 128]
 
-    def sent_proj(d, carry):
-        opp_copy(d).wait_send()
-
-        @pl.when(d > 0)
-        def _():
-            own_copy(d).wait_send()
-        return carry
-
-    def sent_hops(s, carry):
-        for i in range(SUB):
-            hop(s, i).wait_send()
-        share(s + 1).wait_send()
-        return carry
-
-    def sent_back(d, carry):
-        back_copy(d).wait_send()
-        return carry
-
-    def sent_part(d, carry):
-        part_copy(d).wait_send()
-        return carry
-
-    lax.fori_loop(0, NM, sent_proj, 0)
-    share_half(0, 0).wait_send()
-    lax.fori_loop(0, last, sent_hops, 0)
-    for i in range(SUB // 2):
-        last_hop(order(i)).wait_send()
-    share_half(HOPS, 2 * HOPS - 1).wait_send()
-
-    @pl.when(jnp.logical_not(mine))
-    def _():
-        emb_copy(0, 0).wait_send()
-
-    for dy in range(1, NY):
-        emb_copy(0, dy).wait_send()
-    for dy in range(NY):
-        emb_copy(1, dy).wait_send()
-    strip_copy.wait_send()
-    grad_all(lambda copy: copy.wait_send())
-    lax.fori_loop(1, 2 * NM, sent_back, 0)
-    lax.fori_loop(1, NZ, sent_part, 0)
-
 
 def per_device(features, head, caption_ids):
     vmem = pl.BlockSpec(memory_space=pltpu.VMEM)
@@ -438,10 +482,12 @@
     out = pl.pallas_call(
         kernel,
         out_shape=jax.ShapeDtypeStruct((STRIP, COLS), F32),
-        in_specs=[vmem] * 3,
+        in_specs=[pl.BlockSpec(memory_space=pl.ANY)] * 3,
         out_specs=vmem,
         scratch_shapes=[
-            pltpu.VMEM((ROWS, 256), F32),
+            pltpu.VMEM((ROWS, D), BF16),
+            pltpu.VMEM((256, D), BF16),
+            pltpu.VMEM((128, 128), jnp.int32),
             pltpu.VMEM((NM, SL, 256), BF16),
             pltpu.VMEM((NM, SL, 256), BF16),
             pltpu.VMEM((NM, SL, 256), BF16),
@@ -458,8 +504,11 @@
             pltpu.VMEM((NZ * PAD, ROWS), BF16),
             pltpu.VMEM((NM, SL, 256), BF16),
             pltpu.VMEM((2 * NM, SL, 256), BF16),
-            pltpu.VMEM((NZ, 32, 128), BF16),
-            pltpu.VMEM((NZ, 32, 128), BF16),
+            pltpu.VMEM((GROUP, GROUPS, 32, 128), BF16),
+            pltpu.VMEM((GROUP - 1, GROUPS, 32, 128), BF16),
+            pltpu.VMEM((GROUPS, 32, 128), BF16),
+            pltpu.VMEM((GROUPS, 32, 128), BF16),
+            DMA((3,)),
             DMA((2, NM)), DMA((2, NM)),
             DMA((2, NY)), DMA((2, NY)),
             DMA((HOPS, SUB)), DMA((HOPS, SUB)),
@@ -467,13 +516,14 @@
             DMA, DMA,
             DMA((2, NY)), DMA((2, NY)),
             DMA((2 * NM,)), DMA((2 * NM,)),
-            DMA((NZ,)), DMA((NZ,)),
+            DMA((GROUP,)), DMA((GROUP,)),
+            DMA((GROUPS,)), DMA((GROUPS,)),
         ],
         compiler_params=pltpu.CompilerParams(
-            collective_id=0, has_side_effects=True, vmem_limit_bytes=40 << 20
+            collective_id=0, has_side_effects=True, vmem_limit_bytes=63 << 20
         ),
         cost_estimate=pl.CostEstimate(flops=flops, bytes_accessed=2 << 20, transcendentals=ROWS * NZ * CH),
-    )(features[0], head[0], caption_ids.reshape(128, 128))
+    )(features[0], head[0].T, caption_ids.reshape(128, 128))
     return out[None]
 
 

time: 129 us -> 115 us (0.89)
  Pallas kernels: 126 us -> 113 us
    pallas_call x1, Pallas kernels: 126 us -> 113 us  [per_device(): pl.pallas_call(kernel, out_shape=jax.ShapeDtypeStruct((STRIP, COLS), F32)...]
where the time goes in v2:
time: 115 us; the launch traced here: 114 us
  Pallas kernels  113 us (98%)
  local copies, waits for them, and re-layouts  1.36 us (1%)
    pallas_call x1, Pallas kernels, per_device(): pl.pallas_call(kernel, out_shape=jax.ShapeDtypeStruct((STRIP, COLS), F32)...  113 us

profile of v2, /device:TPU:24, one launch (start us, length us, event | category | flops | bytes accessed | tf_op | source)
XLA Modules:
  0.0 114.0 jit_solution(14442968764449158673)
XLA Ops:
  0.0 112.6 %shard_map.37 = f32[18,144]{1,0:T(8,128)} custom-call(bf16[256,1152]{1,0:T(8,128)(2,1)} %bitcast.7, bf16[144,1152]{1,0:T(8,128)(2,1)} %bitcast.8, s32[128,128]{1,0:T(8,128)} %bitcast.9), custom_call_target="tpu_custom_call" | custom-call | flops 2702180352 | bytes 2097152 | tf_op jit(solution)/shard_map/pallas_call | solution.py:482
  112.6 1.4 %copy.4 = f32[1,18,144]{2,0,1:T(1,128)} copy(f32[1,18,144]{2,1,0:T(8,128)} %bitcast.6) | data formatting | bytes 20736 | tf_op jit(solution)/shard_map/broadcast_in_dim | solution.py:527

commit v3 on v2

--- a/solution.py
+++ b/solution.py
@@ -22,7 +22,7 @@
 SUB = 4
 SR = CH // SUB
 HOPS = NZ // 2
-JUMP = 4
+JUMP = 8
 GROUP = 4
 GROUPS = NZ // GROUP
 INV = E ** -0.5
@@ -71,7 +71,7 @@
         return carry
 
     def greet_tower(j, carry):
-        greet(at(1 - k, z, xh, j))
+        greet(at(1 - k, z, c, j))
         return carry
 
     greet(after)
@@ -98,7 +98,8 @@
 
     def opp_copy(d):
         j = lax.rem(m + d, NM)
-        return copy_to(pieces.at[j], opp_in.at[m], proj_s.at[0, d], proj_r.at[0, d], at(1 - k, z, xh, j))
+        return copy_to(pieces.at[j], opp_in.at[m], proj_s.at[0, d], proj_r.at[0, d],
+                       at(1 - k, z, lax.rem(j, 2), (j // 2) * 2 + xh))
 
     def own_copy(d):
         j = lax.rem(m + d, NM)
@@ -117,17 +118,16 @@
     own_in[m] = pieces[m]
 
     lane = lax.broadcasted_iota(jnp.int32, (1, 128), 1)
-    odd = lax.rem(y, 2) == 1
-
-    def id_row(plane):
-        return ids_in[pl.ds(plane * 4 + xh * 2 + y // 2, 1), :]
+    quarter = lax.rem(2 * y + xh, 4) * SL
 
     def fill_ids(p, carry):
-        left = id_row(lax.rem(z + p, NZ))
-        right = id_row(lax.rem(z + NZ - 1 - p, NZ))
-        low = jnp.where(odd, pltpu.roll(left, 64, 1), left)
-        high = jnp.where(odd, right, pltpu.roll(right, 64, 1))
-        opp_ids[pl.ds(p, 1), :] = jnp.where(lane < 64, low, high)
+        row = jnp.zeros((1, 128), jnp.int32)
+        for place in range(4):
+            plane = lax.rem(z + p, NZ) if place < 2 else lax.rem(z + NZ - 1 - p, NZ)
+            some = ids_in[pl.ds(plane * 4 + (place % 2) * 2 + y // 2, 1), :]
+            some = pltpu.roll(some, lax.rem(128 + place * SL - quarter, 128), 1)
+            row = jnp.where(lane // SL == place, some, row)
+        opp_ids[pl.ds(p, 1), :] = row
         return carry
 
     ids_copy.wait()
@@ -135,89 +135,6 @@
     for half in range(2):
         row = ids_in[pl.ds(z * 4 + 2 * c + half, 1), :]
         own_ids[half * 128:(half + 1) * 128, :] = jnp.broadcast_to(row, (128, 128)).T
-
-    def assemble(slots):
-        tiles = [slots[0, :, 0:128]]
-        for t in range(1, NM):
-            tiles.append(slots[t, :, 0:128] + slots[t - 1, :, 128:256])
-        tiles.append(slots[NM - 1, :, 128:256])
-        return jnp.concatenate(tiles, axis=1)
-
-    def norm_of(values):
-        return lax.rsqrt(jnp.mean(values * values, axis=1, keepdims=True) + 1e-06)
-
-    def embed(projected):
-        values = projected.astype(F32)
-        return (values * norm_of(values) * INV).astype(BF16)
-
-    def recv_opp(d, carry):
-        opp_copy(d).wait_recv()
-        return carry
-
-    def recv_own(d, carry):
-        own_copy(d).wait_recv()
-        return carry
-
-    def slot(s):
-        return jnp.maximum(2 * s - 1 + c, 0)
-
-    def hop(s, i):
-        rows = pl.ds(pl.multiple_of(i * SR, SR), SR)
-        return copy_to(ring.at[slot(s), rows], ring.at[slot(s + 1), rows], ring_s.at[s, i], ring_r.at[s, i], after)
-
-    def jump(i):
-        rows = pl.ds(pl.multiple_of(i * SR, SR), SR)
-        return copy_to(ring.at[0, rows], ring.at[slot(JUMP), rows], ring_s.at[JUMP - 1, i], ring_r.at[JUMP - 1, i], ahead)
-
-    def share(s):
-        return copy_to(ring.at[slot(s)], ring.at[slot(s)], sib_s.at[s], sib_r.at[s], sibling)
-
-    def share_half(s, index):
-        rows = pl.ds(pl.multiple_of(c * SL, SL), SL)
-        return copy_to(ring.at[index, rows], ring.at[index, rows], sib_s.at[s], sib_r.at[s], sibling)
-
-    def order(i):
-        return lax.rem(2 * c + i, SUB)
-
-    lax.fori_loop(0, NM, recv_opp, 0)
-    ring[0, pl.ds(pl.multiple_of(c * SL, SL), SL), :] = embed(assemble(opp_in))
-    share_half(0, 0).start()
-    jump(order(0)).start()
-    jump(order(1)).start()
-    hop(0, order(0)).start()
-    hop(0, order(1)).start()
-
-    lax.fori_loop(1, NM, recv_own, 0)
-    own_proj[...] = assemble(own_in)
-    own_rows[...] = embed(own_proj[...])
-
-    share_half(0, 0).wait_recv()
-    jump(order(2)).start()
-    jump(order(3)).start()
-    hop(0, order(2)).start()
-    hop(0, order(3)).start()
-
-    def emb_copy(dx, dy):
-        target = at(k, z, lax.rem(xh + dx, 2), lax.rem(y + dy, NY) * 2 + xh)
-        return copy_to(own_rows, own_emb.at[m], emb_s.at[dx, dy], emb_r.at[c, dy], target)
-
-    def emb_wait(core, dy):
-        copy_to(own_rows, own_emb.at[0], emb_s.at[0, 0], emb_r.at[core, dy], sibling).wait_recv()
-
-    mine = c == xh
-
-    @pl.when(mine)
-    def _():
-        own_emb[m] = own_rows[...]
-
-    @pl.when(jnp.logical_not(mine))
-    def _():
-        emb_copy(0, 0).start()
-
-    for dy in range(1, NY):
-        emb_copy(0, dy).start()
-    for dy in range(NY):
-        emb_copy(1, dy).start()
 
     def strip_columns(half):
         for part in range(3):
@@ -234,9 +151,93 @@
     for part, value in strip_columns(1 - xh):
         strips_out[part * 256:(part + 1) * 256, :] = value
     strip_copy = copy_to(strips_out, strips.at[1], strip_s, strip_r, at(k, z, 1 - xh, m))
-    strip_copy.start()
     for part, value in strip_columns(xh):
         strips[0, part * 256:(part + 1) * 256, :] = value
+
+    def assemble(slots):
+        tiles = [slots[0, :, 0:128]]
+        for t in range(1, NM):
+            tiles.append(slots[t, :, 0:128] + slots[t - 1, :, 128:256])
+        tiles.append(slots[NM - 1, :, 128:256])
+        return jnp.concatenate(tiles, axis=1)
+
+    def norm_of(values):
+        return lax.rsqrt(jnp.mean(values * values, axis=1, keepdims=True) + 1e-06)
+
+    def embed(projected):
+        values = projected.astype(F32)
+        return (values * norm_of(values) * INV).astype(BF16)
+
+    def recv_opp(d, carry):
+        opp_copy(d).wait_recv()
+        return carry
+
+    def recv_own(d, carry):
+        own_copy(d).wait_recv()
+        return carry
+
+    def slot(s):
+        return jnp.maximum(2 * s - 1 + c, 0)
+
+    def hop(s, i):
+        rows = pl.ds(pl.multiple_of(i * SR, SR), SR)
+        return copy_to(ring.at[slot(s), rows], ring.at[slot(s + 1), rows], ring_s.at[s, i], ring_r.at[s, i], after)
+
+    def jump(i):
+        rows = pl.ds(pl.multiple_of(i * SR, SR), SR)
+        return copy_to(ring.at[0, rows], ring.at[slot(JUMP), rows], ring_s.at[JUMP - 1, i], ring_r.at[JUMP - 1, i], ahead)
+
+    def share(s):
+        return copy_to(ring.at[slot(s)], ring.at[slot(s)], sib_s.at[s], sib_r.at[s], sibling)
+
+    def share_half(s, index):
+        rows = pl.ds(pl.multiple_of(c * SL, SL), SL)
+        return copy_to(ring.at[index, rows], ring.at[index, rows], sib_s.at[s], sib_r.at[s], sibling)
+
+    def order(i):
+        return lax.rem(2 * c + i, SUB)
+
+    lax.fori_loop(0, NM, recv_opp, 0)
+    ring[0, pl.ds(pl.multiple_of(c * SL, SL), SL), :] = embed(assemble(opp_in))
+    share_half(0, 0).start()
+    jump(order(0)).start()
+    jump(order(1)).start()
+    hop(0, order(0)).start()
+    hop(0, order(1)).start()
+
+    lax.fori_loop(1, NM, recv_own, 0)
+    own_proj[...] = assemble(own_in)
+    own_rows[...] = embed(own_proj[...])
+
+    share_half(0, 0).wait_recv()
+    jump(order(2)).start()
+    jump(order(3)).start()
+    hop(0, order(2)).start()
+    hop(0, order(3)).start()
+
+    def emb_copy(dx, dy):
+        target = at(k, z, lax.rem(xh + dx, 2), lax.rem(y + dy, NY) * 2 + xh)
+        return copy_to(own_rows, own_emb.at[m], emb_s.at[dx, dy], emb_r.at[c, dy], target)
+
+    def emb_wait(core, dy):
+        copy_to(own_rows, own_emb.at[0], emb_s.at[0, 0], emb_r.at[core, dy], sibling).wait_recv()
+
+    mine = c == xh
+
+    @pl.when(mine)
+    def _():
+        own_emb[m] = own_rows[...]
+
+    @pl.when(jnp.logical_not(mine))
+    def _():
+        emb_copy(0, 0).start()
+
+    for dy in range(1, NY):
+        emb_copy(0, dy).start()
+    for dy in range(NY):
+        emb_copy(1, dy).start()
+
+    strip_copy.start()
     grad[...] = jnp.zeros_like(grad)
 
     def emb_ready():
@@ -253,11 +254,6 @@
         for i in range(SUB):
             hop(s - 1, order(i)).wait_recv()
             hop(s, order(i)).start()
-        share(s).start()
-
-    def end_of_chain(s):
-        for i in range(SUB):
-            hop(s - 1, order(i)).wait_recv()
         share(s).start()
 
     def batch(j):
@@ -272,33 +268,37 @@
         weights = (-sign / (1.0 + jnp.exp(sign * logits))).astype(BF16)
         grad[...] += jnp.dot(weights, opposite, preferred_element_type=F32)
 
-    for t in range(1, JUMP):
-        if t < JUMP - 1:
-            forward(t)
-        else:
-            end_of_chain(t)
+    def arrived(*steps):
+        for step in steps:
+            share(step).wait_recv()
+
+    for t in range(1, 4):
+        forward(t)
         forward(JUMP - 1 + t)
     emb_ready()
-
-    def arrived(j):
-        share(2 * j + 1).wait_recv()
-        share(2 * j + 2).wait_recv()
-
-    def one_hop(t, carry):
+    arrived(1, 2)
+    batch(0)
+    arrived(JUMP)
+
+    def two_hops(u, carry):
+        t = 4 + 2 * u
+        forward(t)
         forward(JUMP - 1 + t)
-        arrived(t - JUMP)
-        batch(t - JUMP)
-        return carry
-
-    def two_hops(u, carry):
-        forward(2 * u + JUMP - 1)
-        arrived(u)
-        batch(u)
-        forward(2 * u + JUMP)
-        return carry
-
-    lax.fori_loop(JUMP, 2 * JUMP, one_hop, 0)
-    lax.fori_loop(JUMP, HOPS // 2 - 2, two_hops, 0)
+        arrived(JUMP + 2 * u + 1, JUMP + 2 * u + 2)
+        batch(JUMP // 2 + u)
+        for i in range(SUB):
+            hop(t, order(i)).wait_recv()
+
+            @pl.when(u == 0)
+            def _(i=i):
+                hop(t + 1, order(i)).start()
+        share(t + 1).start()
+        forward(JUMP + t)
+        arrived(2 * u + 3, 2 * u + 4)
+        batch(1 + u)
+        return carry
+
+    lax.fori_loop(0, 2, two_hops, 0)
 
     last = HOPS - 1
 
@@ -312,8 +312,13 @@
         if i < SUB // 2:
             last_hop(order(i)).start()
     share(last).start()
-    arrived(HOPS // 2 - 2)
-    batch(HOPS // 2 - 2)
+    arrived(JUMP - 1, HOPS - 3, HOPS - 2)
+
+    def left_over(u, carry):
+        batch(JUMP // 2 - 1 + 3 * u)
+        return carry
+
+    lax.fori_loop(0, 2, left_over, 0)
     for i in range(SUB // 2):
         last_hop(order(i)).wait_recv()
     share_half(HOPS, 2 * HOPS - 1).start()
@@ -395,20 +400,42 @@
     r = lax.broadcasted_iota(jnp.int32, (NZ, PAD, 128), 1)
     for g in range(PAD // 8):
         packed = jnp.where(r == STRIP + g, extra[:, g:g + 1, :], packed)
-    part_out[:, :, 0:PAD, :] = packed.astype(BF16).reshape(GROUP, GROUPS, PAD, 128)
-    part_out[:, :, PAD:32, :] = jnp.zeros((GROUP, GROUPS, 32 - PAD, 128), BF16)
+    part_out[...] = packed.reshape(GROUP, GROUPS // 2, 2 * PAD, 128).astype(BF16)
+    sum_out[...] = jnp.zeros_like(sum_out)
 
     low, high = lax.rem(z, GROUP), z // GROUP
 
-    def part_copy(d):
+    stages = ((0, 1), (1, GROUPS // 2 - 1))
+
+    def part_copy(d, stage):
         place = lax.rem(low + d, GROUP)
-        return copy_to(part_out.at[place], part_in.at[d - 1], part_s.at[d], part_r.at[d],
+        pairs = pl.ds(*stages[stage])
+        return copy_to(part_out.at[place, pairs], part_in.at[d - 1, pairs], part_s.at[d, stage], part_r.at[d, stage],
                        at(k, high * GROUP + place, xh, m))
 
-    def sum_copy(d):
-        place = lax.rem(high + d, GROUPS)
-        return copy_to(sum_out.at[place], sum_in.at[d], sum_s.at[d], sum_r.at[d],
-                       at(k, place * GROUP + low, xh, m))
+    def send_parts(stage):
+        for d in (2, 1, 3):
+            part_copy(d, stage).start()
+
+    def add_parts(stage):
+        first, count = stages[stage]
+        for d in (1, 3, 2):
+            part_copy(d, stage).wait_recv()
+        summed = part_out[low, first:first + count].astype(F32)
+        for d in range(GROUP - 1):
+            summed = summed + part_in[d, first:first + count].astype(F32)
+        sum_out[2 * first:2 * (first + count), 0:PAD, :] = summed.reshape(2 * count, PAD, 128).astype(BF16)
+
+    def sum_copy(group):
+        return copy_to(sum_out.at[group], sum_in.at[high], sum_s.at[group], sum_r.at[high],
+                       at(k, group * GROUP + low, xh, m))
+
+    def sum_wait(group):
+        copy_to(sum_out.at[group], sum_in.at[group], sum_s.at[group], sum_r.at[group], sibling).wait_recv()
+
+    def others(groups, act):
+        for group in groups:
+            pl.when(group != high)(lambda group=group: act(group))
 
     def sent_proj(d, carry):
         opp_copy(d).wait_send()
@@ -428,8 +455,12 @@
         back_copy(d).wait_send()
         return carry
 
-    for d in (2, 1, 3):
-        part_copy(d).start()
+    send_parts(0)
+    send_parts(1)
+    add_parts(0)
+    others((0, 1), lambda group: sum_copy(group).start())
+    add_parts(1)
+    others(range(2, GROUPS), lambda group: sum_copy(group).start())
     lax.fori_loop(0, NM, sent_proj, 0)
     share_half(0, 0).wait_send()
     lax.fori_loop(0, last, sent_hops, 0)
@@ -448,23 +479,15 @@
     strip_copy.wait_send()
     grad_all(lambda copy: copy.wait_send())
     lax.fori_loop(1, 2 * NM, sent_back, 0)
-    own_part = part_out[low].astype(F32)
-    for d in (1, 3, 2):
-        part_copy(d).wait_recv()
-    summed = own_part
-    for d in range(GROUP - 1):
-        summed = summed + part_in[d].astype(F32)
-    sum_out[...] = summed.astype(BF16)
-    for d in (4, 3, 5, 2, 6, 1, 7):
-        sum_copy(d).start()
-    for d in range(1, GROUP):
-        part_copy(d).wait_send()
-    for d in range(1, GROUPS):
-        sum_copy(d).wait_send()
-    total = sum_out[high].astype(F32)
-    for d in (1, 7, 2, 6, 3, 5, 4):
-        sum_copy(d).wait_recv()
-        total = total + sum_in[d].astype(F32)
+    for stage in range(2):
+        for d in range(1, GROUP):
+            part_copy(d, stage).wait_send()
+    sum_in[high] = sum_out[high]
+    others(range(GROUPS), sum_wait)
+    total = sum_in[0].astype(F32)
+    for group in range(1, GROUPS):
+        total = total + sum_in[group].astype(F32)
+    others(range(GROUPS), lambda group: sum_copy(group).wait_send())
     out_ref[:, 0:128] = total[0:STRIP, :]
     spread = jnp.concatenate(
         [jnp.broadcast_to(total[STRIP + g:STRIP + g + 1, :], (8, 128)) for g in range(PAD // 8)], axis=0
@@ -504,8 +527,8 @@
             pltpu.VMEM((NZ * PAD, ROWS), BF16),
             pltpu.VMEM((NM, SL, 256), BF16),
             pltpu.VMEM((2 * NM, SL, 256), BF16),
-            pltpu.VMEM((GROUP, GROUPS, 32, 128), BF16),
-            pltpu.VMEM((GROUP - 1, GROUPS, 32, 128), BF16),
+            pltpu.VMEM((GROUP, GROUPS // 2, 2 * PAD, 128), BF16),
+            pltpu.VMEM((GROUP - 1, GROUPS // 2, 2 * PAD, 128), BF16),
             pltpu.VMEM((GROUPS, 32, 128), BF16),
             pltpu.VMEM((GROUPS, 32, 128), BF16),
             DMA((3,)),
@@ -516,7 +539,7 @@
             DMA, DMA,
             DMA((2, NY)), DMA((2, NY)),
             DMA((2 * NM,)), DMA((2 * NM,)),
-            DMA((GROUP,)), DMA((GROUP,)),
+            DMA((GROUP, 2)), DMA((GROUP, 2)),
             DMA((GROUPS,)), DMA((GROUPS,)),
         ],
         compiler_params=pltpu.CompilerParams(

time: 115 us -> 112 us (0.974)
  Pallas kernels: 113 us -> 111 us
    pallas_call x1, Pallas kernels: 113 us -> 111 us  [per_device(): pl.pallas_call(kernel, out_shape=jax.ShapeDtypeStruct((STRIP, COLS), F32)...]
where the time goes in v3:
time: 112 us
  Pallas kernels  111 us (99%)
  local copies, waits for them, and re-layouts  1.36 us (1%)
    pallas_call x1, Pallas kernels, per_device(): pl.pallas_call(kernel, out_shape=jax.ShapeDtypeStruct((STRIP, COLS), F32)...  111 us

profile of v3, /device:TPU:24, one launch (start us, length us, event | category | flops | bytes accessed | tf_op | source)
XLA Modules:
  0.0 112.0 jit_solution(2233446939450856745)
XLA Ops:
  0.0 110.7 %shard_map.37 = f32[18,144]{1,0:T(8,128)} custom-call(bf16[256,1152]{1,0:T(8,128)(2,1)} %bitcast.7, bf16[144,1152]{1,0:T(8,128)(2,1)} %bitcast.8, s32[128,128]{1,0:T(8,128)} %bitcast.9), custom_call_target="tpu_custom_call" | custom-call | flops 2702180352 | bytes 2097152 | tf_op jit(solution)/shard_map/pallas_call | solution.py:505
  110.7 1.4 %copy.4 = f32[1,18,144]{2,0,1:T(1,128)} copy(f32[1,18,144]{2,1,0:T(8,128)} %bitcast.6) | data formatting | bytes 20736 | tf_op jit(solution)/shard_map/broadcast_in_dim | solution.py:550
